TPU v7x, 512 devices: a whole 4x8x8 slice. The times are simulated.
512 devices in a mesh: seq: 128 (over z, y_lo, x, core), dp: 4 (over y_hi).
Axes of the slice: x: 4, y: 8 (y_hi: 4, y_lo: 2; y = y_hi * 2 + y_lo), z: 8, core: 2. Of those that a mesh axis runs over, the one named last changes fastest.
Arguments:
- values: bfloat16 [4, 16384, 4096], P('dp', 'seq'), may hold values from -6 to 6
- cotangent: bfloat16 [4, 16384, 4096], P('dp', 'seq'), may hold values from -6 to 6
- long_filter: bfloat16 [4096, 16384], P(('seq', 'dp')), may hold values from -2 to 2
- bypass: bfloat16 [4096], P(('seq', 'dp')), may hold values from 0.25 to 2
Outputs:
- grad_values: bfloat16 [4, 16384, 4096], P('dp', 'seq')
- grad_filter: float32 [4096, 16384], P(('seq', 'dp'))
- grad_bypass: float32 [4096], P(('seq', 'dp'))
All inputs are finite; a program needn't handle non-finite values.
Results may differ from a plain program's by a relative error of at most 0.01.
Values may be sent and summed in bfloat16 or wider, within the bound.
A program may use at most 128 MiB of HBM per device.

v0:
```python
import math

import jax
import jax.numpy as jnp
from jax import lax
from jax.sharding import PartitionSpec as P

split_radix = 256


def dft_table(points, orient):
    positions = jnp.arange(points, dtype=jnp.int32)
    product = positions[:, None] * positions[None, :] % points
    angles = 2.0 * math.pi / points * product.astype(jnp.float32)
    return (jnp.cos(angles).astype(jnp.bfloat16), (orient * jnp.sin(angles)).astype(jnp.bfloat16))


def twiddle(rows_count, cols_count, points, orient):
    row_index = jnp.arange(rows_count, dtype=jnp.int32)[:, None]
    col_index = jnp.arange(cols_count, dtype=jnp.int32)[None, :]
    angles = 2.0 * math.pi / points * (row_index * col_index % points).astype(jnp.float32)
    return (jnp.cos(angles), orient * jnp.sin(angles))


def contract(form, table, data):
    return jnp.einsum(form, table, data, preferred_element_type=jnp.float32)


def is_direct(points):
    return points <= 128 or points % split_radix != 0


def forward(real_part, imag_part):
    points = real_part.shape[-1]
    table_real, table_imag = dft_table(points, -1.0)
    out_real = contract("nk,...n->...k", table_real, real_part)
    out_imag = contract("nk,...n->...k", table_imag, real_part)
    out_real = out_real - contract("nk,...n->...k", table_imag, imag_part)
    out_imag = out_imag + contract("nk,...n->...k", table_real, imag_part)
    return (out_real.astype(jnp.bfloat16), out_imag.astype(jnp.bfloat16))


def forward_padded(rows):
    length = rows.shape[-1]
    points = 2 * length
    leading = rows.shape[:-1]
    inner_points = points // split_radix
    half_radix = split_radix // 2
    table_real, table_imag = dft_table(split_radix, -1.0)
    split_real = rows.reshape(leading + (half_radix, inner_points))
    section_real = contract("ak,...ab->...kb", table_real[:half_radix], split_real)
    section_imag = contract("ak,...ab->...kb", table_imag[:half_radix], split_real)
    turn_real, turn_imag = twiddle(split_radix, inner_points, points, -1.0)
    moved_real = (section_real * turn_real - section_imag * turn_imag).astype(jnp.bfloat16)
    moved_imag = (section_real * turn_imag + section_imag * turn_real).astype(jnp.bfloat16)
    out_real, out_imag = forward(moved_real, moved_imag)
    return (out_real.reshape(leading + (points,)), out_imag.reshape(leading + (points,)))


def inverse(real_part, imag_part):
    points = real_part.shape[-1]
    leading = real_part.shape[:-1]
    if is_direct(points):
        table_real, table_imag = dft_table(points, 1.0)
        out_real = contract("nk,...n->...k", table_real, real_part) - contract(
            "nk,...n->...k", table_imag, imag_part
        )
        out_imag = contract("nk,...n->...k", table_imag, real_part) + contract(
            "nk,...n->...k", table_real, imag_part
        )
        return (out_real, out_imag)
    inner_points = points // split_radix
    blocked = leading + (split_radix, inner_points)
    inner_real, inner_imag = inverse(real_part.reshape(blocked), imag_part.reshape(blocked))
    turn_real, turn_imag = twiddle(split_radix, inner_points, points, 1.0)
    moved_real = (inner_real * turn_real - inner_imag * turn_imag).astype(jnp.bfloat16)
    moved_imag = (inner_real * turn_imag + inner_imag * turn_real).astype(jnp.bfloat16)
    table_real, table_imag = dft_table(split_radix, 1.0)
    out_real = contract("ka,...kb->...ab", table_real, moved_real) - contract(
        "ka,...kb->...ab", table_imag, moved_imag
    )
    return (out_real.reshape(leading + (points,)), None)


def conj_wide(first_real, first_imag, second_real, second_imag):
    first_real = first_real.astype(jnp.float32)
    first_imag = first_imag.astype(jnp.float32)
    second_real = second_real.astype(jnp.float32)
    second_imag = second_imag.astype(jnp.float32)
    return (
        first_real * second_real + first_imag * second_imag,
        first_real * second_imag - first_imag * second_real,
    )


def summed_products(first, second):
    return jnp.einsum("sck,sck->ck", first, second, preferred_element_type=jnp.float32)


def channel_work(values_rows, cotangent_rows, filter_rows, gain_rows):
    length = values_rows.shape[-1]
    points = 2 * length
    filter_real, filter_imag = forward_padded(filter_rows)
    values_real, values_imag = forward_padded(values_rows)
    cotangent_real, cotangent_imag = forward_padded(cotangent_rows)
    lag_real, lag_imag = conj_wide(filter_real, filter_imag, cotangent_real, cotangent_imag)
    signal = inverse(lag_real.astype(jnp.bfloat16), lag_imag.astype(jnp.bfloat16))[0]
    grad_rows = (
        signal[..., :length] / points
        + gain_rows.astype(jnp.float32)[:, None] * cotangent_rows.astype(jnp.float32)
    ).astype(jnp.bfloat16)
    cross_real = (
        summed_products(values_real, cotangent_real) + summed_products(values_imag, cotangent_imag)
    ).astype(jnp.bfloat16)
    cross_imag = (
        summed_products(values_real, cotangent_imag) - summed_products(values_imag, cotangent_real)
    ).astype(jnp.bfloat16)
    cross_terms = inverse(cross_real, cross_imag)[0][..., :length] / points
    gain_terms = jnp.einsum(
        "scl,scl->c", cotangent_rows, values_rows, preferred_element_type=jnp.float32
    )
    return (grad_rows, cross_terms, gain_terms)


def shards(values, cotangent, long_filter, bypass):
    seq_count = lax.axis_size("seq")
    copies = lax.axis_size("dp")
    tok_rows = values.shape[1]
    length = tok_rows * seq_count
    grad_scale = 1.0 / math.sqrt(copies * length)
    values_moved = jnp.swapaxes(values, 1, 2)
    cotangent_moved = jnp.swapaxes(cotangent, 1, 2)
    values_rows, cotangent_rows = (
        lax.all_to_all(values_moved, "seq", split_axis=1, concat_axis=2, tiled=True),
        lax.all_to_all(cotangent_moved, "seq", split_axis=1, concat_axis=2, tiled=True),
    )
    values_rows, cotangent_rows = (
        lax.all_to_all(values_rows, "dp", split_axis=1, concat_axis=0, tiled=True),
        lax.all_to_all(cotangent_rows, "dp", split_axis=1, concat_axis=0, tiled=True),
    )
    grad_rows, cross_terms, gain_terms = channel_work(
        values_rows, cotangent_rows, long_filter, bypass
    )
    grad_rows = lax.all_to_all(grad_rows, "dp", split_axis=0, concat_axis=1, tiled=True)
    grad_tokens = lax.all_to_all(grad_rows, "seq", split_axis=2, concat_axis=1, tiled=True)
    return (jnp.swapaxes(grad_tokens, 1, 2), cross_terms * grad_scale, gain_terms * grad_scale)


def solution(mesh):
    placed = (P("dp", "seq", None), P("dp", "seq", None), P(("seq", "dp"), None), P(("seq", "dp")))
    return jax.shard_map(
        shards,
        mesh=mesh,
        in_specs=placed,
        out_specs=(P("dp", "seq", None), P(("seq", "dp"), None), P(("seq", "dp"))),
        check_vma=False,
    )
```

profile of v0, /device:TPU:1, one launch (start us, length us, event | category | flops | bytes accessed | tf_op | source)
XLA Modules:
  0.0 510.0 jit_solution(3409563824395897368)
XLA Ops:
  0.6 5.6 %copy.88 = bf16[1,128,4096]{1,0,2:T(2,128)(2,1)} copy(bf16[1,128,4096]{2,1,0:T(8,128)(2,1)} %param.4) | data formatting | bytes 2097152 | tf_op args[0]
  10.5 22.4 %reduce.14 = bf16[4096,128]{1,0:T(8,128)(2,1)S(1)} reduce(bf16[4096,1,128]{2,1,0:T(2,128)(2,1)S(1)} %bitcast_bitcast_fusion.1, bf16[]{:T(256)} %broadcast.461), dimensions={1}, to_apply=%bitcast_bitcast_fusion.1.reduce_sub_computation | reduce | bytes 2097154
  34.0 17.0 %all-to-all-start.4 = ((bf16[128,2,2048]{2,1,0:T(2,128)(2,1)}), bf16[128,2,2048]{2,1,0:T(2,128)(2,1)S(1)}, u32[]{:S(2)}, u32[]{:S(2)}) async-start(bf16[128,2,2048]{2,1,0:T(2,128)(2,1)} %reshape.213), calls=%async_computation.4 | async-start | bytes 2097152 | tf_op jit(solution)/shard_map/all_to_all | solution.py:134
  58.7 23.4 %reduce.16 = bf16[4096,128]{1,0:T(8,128)(2,1)} reduce(bf16[4096,1,128]{2,1,0:T(2,128)(2,1)S(1)} %bitcast_bitcast_fusion.2, bf16[]{:T(256)} %broadcast.461), dimensions={1}, to_apply=%bitcast_bitcast_fusion.2.reduce_sub_computation | reduce | bytes 2097154
  85.2 12.9 %all-to-all-start = ((bf16[128,2,2048]{2,1,0:T(2,128)(2,1)}), bf16[128,2,2048]{2,1,0:T(2,128)(2,1)S(1)}, u32[]{:S(2)}, u32[]{:S(2)}) async-start(bf16[128,2,2048]{2,1,0:T(2,128)(2,1)} %reshape.207), calls=%async_computation | async-start | bytes 2097152 | tf_op jit(solution)/shard_map/all_to_all | solution.py:135
  98.2 6.5 %reshape.214 = bf16[4096,1,128]{2,1,0:T(2,128)(2,1)S(1)} reshape(bf16[128,2,2048]{2,1,0:T(2,128)(2,1)} %copy-done.23) | data formatting | bytes 2097152
  110.2 8.0 %reduce.15 = bf16[32,16384]{1,0:T(8,128)(2,1)} reduce(bf16[32,1,16384]{2,1,0:T(2,128)(2,1)S(1)} %bitcast.239, bf16[]{:T(256)} %broadcast.461), dimensions={1}, to_apply=%bitcast.198.reduce_sub_computation | reduce | bytes 2097154
  126.9 6.1 %all-to-all-start.5 = ((bf16[4,2,65536]{2,1,0:T(2,128)(2,1)}), bf16[4,2,65536]{2,1,0:T(2,128)(2,1)}, u32[]{:S(2)}, u32[]{:S(2)}) async-start(bf16[4,2,65536]{2,1,0:T(2,128)(2,1)} %reshape.215), calls=%async_computation.5 | async-start | bytes 2097152 | tf_op jit(solution)/shard_map/all_to_all | solution.py:138
  138.9 6.5 %reshape.208 = bf16[4096,1,128]{2,1,0:T(2,128)(2,1)S(1)} reshape(bf16[128,2,2048]{2,1,0:T(2,128)(2,1)} %copy-done.22) | data formatting | bytes 2097152
  151.1 8.0 %reduce.17 = bf16[32,16384]{1,0:T(8,128)(2,1)} reduce(bf16[32,1,16384]{2,1,0:T(2,128)(2,1)S(1)} %bitcast.240, bf16[]{:T(256)} %broadcast.461), dimensions={1}, to_apply=%bitcast.192.reduce_sub_computation | reduce | bytes 2097154
  163.1 6.9 %all-to-all-start.1 = ((bf16[4,2,65536]{2,1,0:T(2,128)(2,1)}), bf16[4,2,65536]{2,1,0:T(2,128)(2,1)}, u32[]{:S(2)}, u32[]{:S(2)}) async-start(bf16[4,2,65536]{2,1,0:T(2,128)(2,1)} %reshape.209), calls=%async_computation.1 | async-start | bytes 2097152 | tf_op jit(solution)/shard_map/all_to_all | solution.py:139
  174.7 6.2 %bitcast_reduce_fusion = bf16[32,16384]{1,0:T(8,128)(2,1)S(1)} fusion(bf16[32,1,16384]{2,1,0:T(2,128)(2,1)S(1)} %reshape.216), kind=kLoop, calls=%fused_computation.282 | loop fusion | bytes 2097152 | tf_op jit(solution)/shard_map/all_to_all | solution.py:138
  191.1 7.1 %bitcast_reduce_fusion.1 = bf16[32,16384]{1,0:T(8,128)(2,1)} fusion(bf16[32,1,16384]{2,1,0:T(2,128)(2,1)S(1)} %reshape.210), kind=kLoop, calls=%fused_computation.283 | loop fusion | bytes 2097152 | tf_op jit(solution)/shard_map/all_to_all | solution.py:139
  200.3 5.3 %fusion.12 = (bf16[4,8,256,128]{3,2,1,0:T(8,128)(2,1)}, bf16[4,8,256,128]{3,2,1,0:T(8,128)(2,1)S(1)}, bf16[4,8,256,128]{3,2,1,0:T(8,128)(2,1)S(1)}, bf16[4,8,256,128]{3,2,1,0:T(8,128)(2,1)S(1)}) fusion(f32[256,4,8,128]{3,0,2,1:T(8,128)S(1)} %copy-done.15, f32[256,4,8,128]{3,0,2,1:T(8,128)S(1)} %copy-done.14, f32[256,128]{1,0:T(8,128)S(1)} %copy-done.28, ...), kind=kOutput, calls=%fused_computation.33 | convolution fusion | flops 285212672 | bytes 22347776 | tf_op jit(solution)/shard_map/ak,...ab->...kb/dot_general | solution.py:26
  253.8 7.4 %fusion.7 = (f32[8,32768]{1,0:T(8,128)}, f32[8,32768]{1,0:T(8,128)S(1)}, f32[8,32768]{1,0:T(8,128)}, f32[8,32768]{1,0:T(8,128)S(1)}) fusion(bf16[4,8,32768]{2,1,0:T(8,128)(2,1)} %reshape.171, bf16[4,8,32768]{2,1,0:T(8,128)(2,1)} %reshape.170, bf16[4,8,32768]{2,1,0:T(8,128)(2,1)} %reshape.169, bf16[4,8,32768]{2,1,0:T(8,128)(2,1)} %reshape.172), kind=kLoop, calls=%fused_computation.15 | loop fusion | flops 11534336 | bytes 12582912 | tf_op jit(solution)/shard_map/sck,sck->ck/dot_general | solution.py:97
  272.8 5.4 %copy.84 = f32[4,8,256,128]{3,2,1,0:T(8,128)} copy(f32[4,8,256,128]{2,3,1,0:T(8,128)} %subtract_bitcast_fusion) | data formatting | bytes 8388608 | tf_op jit(solution)/shard_map/sub | solution.py:79
  287.2 7.5 %all-to-all-start.2 = ((bf16[4,8,16384]{2,1,0:T(8,128)(2,1)}), bf16[4,8,16384]{2,1,0:T(8,128)(2,1)}, u32[]{:S(2)}, u32[]{:S(2)}) async-start(bf16[4,8,16384]{2,1,0:T(8,128)(2,1)} %fusion.14), calls=%async_computation.2 | async-start | bytes 2097152 | tf_op jit(solution)/shard_map/all_to_all | solution.py:144
  309.3 16.0 %copy.85 = bf16[1,32,16384]{1,0,2:T(2,128)(2,1)} copy(bf16[1,32,16384]{2,1,0:T(8,128)(2,1)} %bitcast.37) | data formatting | bytes 2097152 | tf_op jit(solution)/shard_map/all_to_all | solution.py:144
  325.3 90.9 %reduce.18 = bf16[16384,32]{1,0:T(8,128)(2,1)} reduce(bf16[16384,1,32]{2,1,0:T(2,128)(2,1)} %bitcast.228, bf16[]{:T(256)} %broadcast.461), dimensions={1}, to_apply=%bitcast.194.reduce_sub_computation | reduce | bytes 2097154
  416.2 7.3 %reshape.211 = bf16[128,2,2048]{2,1,0:T(2,128)(2,1)} reshape(bf16[16384,32]{1,0:T(8,128)(2,1)} %reduce.18) | data formatting | bytes 2097152
  423.6 25.5 %all-to-all-start.3 = ((bf16[128,2,2048]{2,1,0:T(2,128)(2,1)}), bf16[128,2,2048]{2,1,0:T(2,128)(2,1)S(1)}, u32[]{:S(2)}, u32[]{:S(2)}) async-start(bf16[128,2,2048]{2,1,0:T(2,128)(2,1)} %reshape.211), calls=%async_computation.3 | async-start | bytes 2097152 | tf_op jit(solution)/shard_map/all_to_all | solution.py:145
  449.9 28.3 %all-to-all-done.3 = bf16[128,2,2048]{2,1,0:T(2,128)(2,1)S(1)} async-done(((bf16[128,2,2048]{2,1,0:T(2,128)(2,1)}), bf16[128,2,2048]{2,1,0:T(2,128)(2,1)S(1)}, u32[]{:S(2)}, u32[]{:S(2)}) %all-to-all-start.3) | async-done | bytes 1048608 | tf_op jit(solution)/shard_map/all_to_all | solution.py:145
  478.3 14.1 %reshape.212 = bf16[16384,1,32]{2,1,0:T(2,128)(2,1)} reshape(bf16[128,2,2048]{2,1,0:T(2,128)(2,1)S(1)} %all-to-all-done.3) | data formatting | bytes 2097152
  492.3 15.1 %copy.86 = bf16[1,32,16384]{2,1,0:T(8,128)(2,1)S(1)} copy(bf16[1,32,16384]{1,0,2:T(2,128)(2,1)} %bitcast.229) | data formatting | bytes 2097152 | tf_op jit(solution)/shard_map/all_to_all | solution.py:145
  (136 shorter events, 149.1 us)
Async XLA Ops:
  0.6 136.0 %copy-start = (bf16[8,16384]{1,0:T(8,128)(2,1)S(1)}, bf16[8,16384]{1,0:T(8,128)(2,1)}, u32[]{:S(2)}) copy-start(bf16[8,16384]{1,0:T(8,128)(2,1)} %param.6) | copy-start | bytes 786436
  32.9 18.2 %copy-start.29 = (bf16[1,128,4096]{2,1,0:T(8,128)(2,1)S(1)}, bf16[1,128,4096]{2,1,0:T(8,128)(2,1)}, u32[]{:S(2)}) copy-start(bf16[1,128,4096]{2,1,0:T(8,128)(2,1)} %param.5) | copy-start | bytes 3145732
  34.0 50.2 %all-to-all-start.4 = ((bf16[128,2,2048]{2,1,0:T(2,128)(2,1)}), bf16[128,2,2048]{2,1,0:T(2,128)(2,1)S(1)}, u32[]{:S(2)}, u32[]{:S(2)}) async-start(bf16[128,2,2048]{2,1,0:T(2,128)(2,1)} %reshape.213), calls=%async_computation.4 | async-start | bytes 2097152 | tf_op jit(solution)/shard_map/all_to_all | solution.py:134
  58.7 39.4 %copy-start.31 = (bf16[8]{0:T(256)(128)(2,1)S(1)}, bf16[8]{0:T(256)(128)(2,1)}, u32[]{:S(2)}) copy-start(bf16[8]{0:T(256)(128)(2,1)} %param.7) | copy-start | bytes 52
  85.2 41.7 %all-to-all-start = ((bf16[128,2,2048]{2,1,0:T(2,128)(2,1)}), bf16[128,2,2048]{2,1,0:T(2,128)(2,1)S(1)}, u32[]{:S(2)}, u32[]{:S(2)}) async-start(bf16[128,2,2048]{2,1,0:T(2,128)(2,1)} %reshape.207), calls=%async_computation | async-start | bytes 2097152 | tf_op jit(solution)/shard_map/all_to_all | solution.py:135
  126.9 11.1 %copy-start.22 = (bf16[128,2,2048]{2,1,0:T(2,128)(2,1)}, bf16[128,2,2048]{2,1,0:T(2,128)(2,1)S(1)}, u32[]{:S(2)}) copy-start(bf16[128,2,2048]{2,1,0:T(2,128)(2,1)S(1)} %all-to-all-done) | copy-start | bytes 3145732
  126.9 36.2 %all-to-all-start.5 = ((bf16[4,2,65536]{2,1,0:T(2,128)(2,1)}), bf16[4,2,65536]{2,1,0:T(2,128)(2,1)}, u32[]{:S(2)}, u32[]{:S(2)}) async-start(bf16[4,2,65536]{2,1,0:T(2,128)(2,1)} %reshape.215), calls=%async_computation.5 | async-start | bytes 2097152 | tf_op jit(solution)/shard_map/all_to_all | solution.py:138
  159.1 10.9 %copy-start.21 = (bf16[8,256,128]{2,1,0:T(8,128)(2,1)S(1)}, bf16[8,256,128]{2,1,0:T(8,128)(2,1)}, u32[]{:S(2)}) copy-start(bf16[8,256,128]{2,1,0:T(8,128)(2,1)} %copy-done.20) | copy-start | bytes 1572868
  159.1 11.4 %copy-start.19 = (bf16[8,256,128]{2,1,0:T(8,128)(2,1)S(1)}, bf16[8,256,128]{2,1,0:T(8,128)(2,1)}, u32[]{:S(2)}) copy-start(bf16[8,256,128]{2,1,0:T(8,128)(2,1)} %copy-done.18) | copy-start | bytes 1572868
  163.1 24.9 %all-to-all-start.1 = ((bf16[4,2,65536]{2,1,0:T(2,128)(2,1)}), bf16[4,2,65536]{2,1,0:T(2,128)(2,1)}, u32[]{:S(2)}, u32[]{:S(2)}) async-start(bf16[4,2,65536]{2,1,0:T(2,128)(2,1)} %reshape.209), calls=%async_computation.1 | async-start | bytes 2097152 | tf_op jit(solution)/shard_map/all_to_all | solution.py:139
  174.7 9.8 %copy-start.9 = (bf16[32,1,16384]{2,1,0:T(2,128)(2,1)}, bf16[32,1,16384]{2,1,0:T(2,128)(2,1)S(1)}, u32[]{:S(2)}) copy-start(bf16[32,1,16384]{2,1,0:T(2,128)(2,1)S(1)} %reshape.216) | copy-start | bytes 3145732
  174.7 9.8 %copy-start.26 = (f32[256,256]{0,1:T(8,128)S(1)}, f32[256,256]{0,1:T(8,128)}, u32[]{:S(2)}) copy-start(f32[256,256]{0,1:T(8,128)} %copy-done.25) | copy-start | bytes 786436
  191.1 9.1 %copy-start.4 = (bf16[32,1,16384]{2,1,0:T(2,128)(2,1)}, bf16[32,1,16384]{2,1,0:T(2,128)(2,1)S(1)}, u32[]{:S(2)}) copy-start(bf16[32,1,16384]{2,1,0:T(2,128)(2,1)S(1)} %reshape.210) | copy-start | bytes 3145732
  191.1 9.1 %copy-start.14 = (f32[256,4,8,128]{3,0,2,1:T(8,128)S(1)}, f32[256,4,8,128]{3,0,2,1:T(8,128)}, u32[]{:S(2)}) copy-start(f32[256,4,8,128]{3,0,2,1:T(8,128)} %fusion.27) | copy-start | bytes 12582916
  191.1 9.1 %copy-start.15 = (f32[256,4,8,128]{3,0,2,1:T(8,128)S(1)}, f32[256,4,8,128]{3,0,2,1:T(8,128)}, u32[]{:S(2)}) copy-start(f32[256,4,8,128]{3,0,2,1:T(8,128)} %fusion.25) | copy-start | bytes 12582916
  205.6 10.1 %copy-start.11 = (bf16[4,8,256,128]{3,2,1,0:T(8,128)(2,1)}, bf16[4,8,256,128]{3,2,1,0:T(8,128)(2,1)S(1)}, u32[]{:S(2)}) copy-start(bf16[4,8,256,128]{3,2,1,0:T(8,128)(2,1)S(1)} %get-tuple-element.26) | copy-start | bytes 6291460
  228.2 5.1 %copy-start.2 = (bf16[4,8,256,128]{3,2,1,0:T(8,128)(2,1)S(1)}, bf16[4,8,256,128]{3,2,1,0:T(8,128)(2,1)}, u32[]{:S(2)}) copy-start(bf16[4,8,256,128]{3,2,1,0:T(8,128)(2,1)} %subtract_convert_fusion.3) | copy-start | bytes 6291460
  228.2 5.1 %copy-start.6 = (f32[8,256,128]{2,1,0:T(8,128)S(1)}, f32[8,256,128]{2,1,0:T(8,128)}, u32[]{:S(2)}) copy-start(f32[8,256,128]{2,1,0:T(8,128)} %fusion.22) | copy-start | bytes 3145732
  233.4 4.3 copy-start.10
  253.8 9.9 %copy-start.13 = (f32[4,8,256,128]{3,2,1,0:T(8,128)S(1)}, f32[4,8,256,128]{3,2,1,0:T(8,128)}, u32[]{:S(2)}) copy-start(f32[4,8,256,128]{3,2,1,0:T(8,128)} %fusion.100) | copy-start | bytes 12582916
  278.2 5.2 %copy-start.5 = (bf16[32,1,16384]{2,1,0:T(2,128)(2,1)S(1)}, bf16[32,1,16384]{2,1,0:T(2,128)(2,1)}, u32[]{:S(2)}) copy-start(bf16[32,1,16384]{2,1,0:T(2,128)(2,1)} %copy-done.4) | copy-start | bytes 3145732
  287.1 10.9 %copy-start.17 = (bf16[1,8,256,128]{3,1,2,0:T(8,128)(2,1)S(1)}, bf16[1,8,256,128]{3,1,2,0:T(8,128)(2,1)}, u32[]{:S(2)}) copy-start(bf16[1,8,256,128]{3,1,2,0:T(8,128)(2,1)} %copy-done.16) | copy-start | bytes 1572868
  287.2 22.2 %all-to-all-start.2 = ((bf16[4,8,16384]{2,1,0:T(8,128)(2,1)}), bf16[4,8,16384]{2,1,0:T(8,128)(2,1)}, u32[]{:S(2)}, u32[]{:S(2)}) async-start(bf16[4,8,16384]{2,1,0:T(8,128)(2,1)} %fusion.14), calls=%async_computation.2 | async-start | bytes 2097152 | tf_op jit(solution)/shard_map/all_to_all | solution.py:144
  423.6 54.7 %all-to-all-start.3 = ((bf16[128,2,2048]{2,1,0:T(2,128)(2,1)}), bf16[128,2,2048]{2,1,0:T(2,128)(2,1)S(1)}, u32[]{:S(2)}, u32[]{:S(2)}) async-start(bf16[128,2,2048]{2,1,0:T(2,128)(2,1)} %reshape.211), calls=%async_computation.3 | async-start | bytes 2097152 | tf_op jit(solution)/shard_map/all_to_all | solution.py:145
  (14 other events, 24.6 us)
where the time goes:
time: 520 us; the launch traced here: 510 us
  other arithmetic  175 us (34%)
  local copies, waits for them, and re-layouts  159 us (31%)
  starting transfers between devices  75.9 us (15%)
  matrix products  64.8 us (12%)
  waiting for transfers between devices  33.9 us (7%)
    unnamed x7, other arithmetic  154 us
    unnamed x84, local copies, waits for them, and re-layouts  76.5 us
    dot_general x30, matrix products, contract(): return jnp.einsum(form, table, data, preferred_element_type=jnp.float32)  64.8 us
    all_to_all x1, waiting for transfers between devices, shards(): lax.all_to_all(grad_rows, 'seq', split_axis=2, concat_axis=1, tiled=True)  28.3 us
    all_to_all x1, starting transfers between devices, shards(): lax.all_to_all(grad_rows, 'seq', split_axis=2, concat_axis=1, tiled=True)  25.5 us
    all_to_all x1, starting transfers between devices, shards(): lax.all_to_all(values_moved, 'seq', split_axis=1, concat_axis=2, tiled=True)  17 us
    all_to_all x1, local copies, waits for them, and re-layouts, shards(): lax.all_to_all(grad_rows, 'dp', split_axis=0, concat_axis=1, tiled=True)  16 us
    all_to_all x3, local copies, waits for them, and re-layouts, shards(): lax.all_to_all(grad_rows, 'seq', split_axis=2, concat_axis=1, tiled=True)  15.9 us
  transfers between devices with their start and end apart: 6, of which 3 were waited for; matrix products, arithmetic and copies ran while one was open for 22% of the time, Pallas kernels for 0%

commit v1 on v0

v1 whole, which is shorter than its diff:
```python
import functools
import math

import jax
import jax.numpy as jnp
import ml_dtypes
import numpy as np
from jax import lax
from jax.experimental import pallas as pl
from jax.experimental.pallas import tpu as pltpu
from jax.sharding import PartitionSpec as P

MESH = pl.DeviceIdType.MESH
lanes = 128
wide = jnp.float32
narrow = jnp.bfloat16


def tables(sources, points):
    whole = 2 * sources * points
    half = np.arange(sources) + 0.5
    outer = 2.0 * np.pi * np.outer(half, np.arange(sources)) / (2 * sources)
    turn = 2.0 * np.pi * np.outer(half, np.arange(points)) / whole
    inner = 2.0 * np.pi * (np.outer(np.arange(points), np.arange(points)) % points) / points
    cos, sin = np.cos(inner), np.sin(inner)
    as_narrow = lambda table: table.astype(ml_dtypes.bfloat16)
    return (
        as_narrow(np.concatenate([np.cos(outer), -np.sin(outer)], 0)),
        as_narrow(np.block([[cos, -sin], [sin, cos]])),
        as_narrow(np.block([[cos, sin], [-sin, cos]])),
        as_narrow(2.0 / whole * np.concatenate([np.cos(outer).T, -np.sin(outer).T], 1)),
        np.stack([np.cos(turn), np.sin(turn)]).astype(np.float32),
    )


def kernel(
    seqs, copies, scale,
    values_ref, cotangent_ref, filter_ref, gain_ref, outer_ref, inner_ref, back_inner_ref, back_outer_ref, turn_ref,
    grad_ref, grad_filter_ref, grad_gain_ref,
    cot_out, val_out, cot_in, val_in, filters, gains, cot_wide, val_wide, cot_spec, filter_spec,
    grad_out, grad_in, part_out, part_in, gain_out, gain_in, send_sem, recv_sem, near_send_sem, near_recv_sem,
):
    me, mine = lax.axis_index("seq"), lax.axis_index("dp")
    points = values_ref.shape[0]
    group = cot_in.shape[1]
    own = filter_ref.shape[0]
    per_tile = lanes // group

    barrier = pltpu.get_barrier_semaphore()

    def greet(step, carry):
        pl.semaphore_signal(barrier, inc=1, device_id={"seq": lax.rem(me + step, seqs)}, device_id_type=MESH)
        return carry

    lax.fori_loop(1, seqs, greet, 0)
    for step in range(1, copies):
        pl.semaphore_signal(barrier, inc=1, device_id={"dp": lax.rem(mine + step, copies)}, device_id_type=MESH)

    def turn_round(tokens_ref, rows_ref):
        def tile(at, carry):
            block = tokens_ref[:, pl.ds(pl.multiple_of(at * lanes, lanes), lanes)]
            rows_ref[pl.ds(at * per_tile, per_tile)] = block.T.reshape(per_tile, group, points)
            return carry

        lax.fori_loop(0, seqs // per_tile, tile, 0, unroll=2)

    def send(rows_ref, there_ref, which):
        def one(step, carry):
            peer = lax.rem(me + step * 17, seqs)
            pltpu.make_async_remote_copy(
                src_ref=rows_ref.at[peer],
                dst_ref=there_ref.at[me],
                send_sem=send_sem.at[which],
                recv_sem=recv_sem.at[which],
                device_id={"seq": peer},
                device_id_type=MESH,
            ).start()
            return carry

        lax.fori_loop(1, seqs, one, 0)
        there_ref[pl.ds(me, 1)] = rows_ref[pl.ds(me, 1)]

    def all_of(rows_ref, there_ref, which):
        return pltpu.make_async_remote_copy(
            src_ref=rows_ref.at[pl.ds(0, seqs - 1)],
            dst_ref=there_ref.at[pl.ds(0, seqs - 1)],
            send_sem=send_sem.at[which],
            recv_sem=recv_sem.at[which],
            device_id={"seq": lax.rem(me + 1, seqs)},
            device_id_type=MESH,
        )

    def near(which, step, src_ref, dst_ref):
        return pltpu.make_async_remote_copy(
            src_ref=src_ref,
            dst_ref=dst_ref,
            send_sem=near_send_sem.at[which, step],
            recv_sem=near_recv_sem.at[which, step],
            device_id={"dp": lax.rem(mine + step, copies)},
            device_id_type=MESH,
        )

    turn_round(cotangent_ref, cot_out)
    pl.semaphore_wait(barrier, seqs + copies - 2)

    filter_copies = []
    for step in range(1, copies):
        filter_copies.append(near(0, step, filter_ref, filters.at[mine]))
        filter_copies.append(near(1, step, gain_ref, gains.at[mine]))
    for copy in filter_copies:
        copy.start()
    filters[pl.ds(mine, 1)] = filter_ref[...][None]
    gains[pl.ds(mine, 1)] = gain_ref[...][None]
    send(cot_out, cot_in, 0)
    turn_round(values_ref, val_out)
    send(val_out, val_in, 1)

    outer, inner = outer_ref[...], inner_ref[...]
    back_inner, back_outer = back_inner_ref[...], back_outer_ref[...]
    dot = functools.partial(jnp.dot, preferred_element_type=wide)

    def rows_of(wide_ref, channel):
        return wide_ref[pl.ds(channel, seqs, stride=group), :]

    def transform(first, second):
        cos, sin = turn_ref[0], turn_ref[1]
        both = dot(outer, jnp.concatenate([first.astype(narrow), second.astype(narrow)], 1))
        turned = []
        for at in range(2):
            real = both[:seqs, at * points : (at + 1) * points]
            imag = both[seqs:, at * points : (at + 1) * points]
            turned.append(
                jnp.concatenate([(real * cos + imag * sin).astype(narrow), (imag * cos - real * sin).astype(narrow)], 1)
            )
        return [dot(part, inner) for part in turned]

    def times_conj(first, second):
        first_real, first_imag = first[:, :points].astype(wide), first[:, points:].astype(wide)
        second_real, second_imag = second[:, :points].astype(wide), second[:, points:].astype(wide)
        return jnp.concatenate(
            [
                (first_real * second_real + first_imag * second_imag).astype(narrow),
                (first_real * second_imag - first_imag * second_real).astype(narrow),
            ],
            1,
        )

    def invert(first, second):
        cos, sin = turn_ref[0], turn_ref[1]
        turned = []
        for spec in (first, second):
            both = dot(spec, back_inner)
            real, imag = both[:, :points], both[:, points:]
            turned.append(
                jnp.concatenate([(real * cos - imag * sin).astype(narrow), (real * sin + imag * cos).astype(narrow)], 0)
            )
        both = dot(back_outer, jnp.concatenate(turned, 1))
        return both[:, :points], both[:, points:]

    for copy in filter_copies:
        copy.wait_recv()

    def widen_filter(at, carry):
        for copy in range(copies):
            val_wide[pl.ds(at * group + copy * own, own), :] = filters[
                copy, :, pl.ds(pl.multiple_of(at * points, points), points)
            ].astype(wide)
        return carry

    lax.fori_loop(0, seqs, widen_filter, 0, unroll=4)

    def filter_pair(pair, carry):
        at = pair * 2
        specs = transform(rows_of(val_wide, at), rows_of(val_wide, at + 1))
        for offset in range(2):
            filter_spec[at + offset] = specs[offset].astype(narrow)
        return carry

    lax.fori_loop(0, group // 2, filter_pair, 0)

    all_of(cot_out, cot_in, 0).wait_recv()

    def widen_cot(at, carry):
        cot_wide[pl.ds(pl.multiple_of(at * group, group), group), :] = cot_in[at].astype(wide)
        return carry

    lax.fori_loop(0, seqs, widen_cot, 0, unroll=4)

    def grad_pair(pair, carry):
        at = pair * 2
        rows = rows_of(cot_wide, at), rows_of(cot_wide, at + 1)
        specs = transform(*rows)
        lags = []
        for offset in range(2):
            spec = specs[offset].astype(narrow)
            cot_spec[at + offset] = spec
            lags.append(times_conj(filter_spec[at + offset], spec))
        signals = invert(*lags)
        for offset in range(2):
            channel = at + offset
            gain = gains[channel // own, pl.ds(lax.rem(channel, own), 1), :]
            cot_wide[pl.ds(channel, seqs, stride=group), :] = signals[offset] + gain * rows[offset]
        return carry

    lax.fori_loop(0, group // 2, grad_pair, 0)

    def pack_grad(at, carry):
        grad_out[at] = cot_wide[pl.ds(pl.multiple_of(at * group, group), group), :].astype(narrow)
        return carry

    lax.fori_loop(0, seqs, pack_grad, 0, unroll=4)
    send(grad_out, grad_in, 2)

    all_of(val_out, val_in, 1).wait_recv()

    def widen_val(at, total):
        block = val_in[at].astype(wide)
        val_wide[pl.ds(pl.multiple_of(at * group, group), group), :] = block
        return total + block * cot_in[at].astype(wide)

    total = lax.fori_loop(0, seqs, widen_val, jnp.zeros((group, points), wide), unroll=4)
    gain_out[...] = total.reshape(copies, own, points)

    def cross_pair(pair, carry):
        at = pair * 2
        specs = transform(rows_of(val_wide, at), rows_of(val_wide, at + 1))
        parts = [times_conj(specs[offset].astype(narrow), cot_spec[at + offset]) for offset in range(2)]
        signals = invert(*parts)
        for offset in range(2):
            val_wide[pl.ds(at + offset, seqs, stride=group), :] = signals[offset]
        return carry

    lax.fori_loop(0, group // 2, cross_pair, 0)

    def pack_part(at, carry):
        for copy in range(copies):
            part_out[copy, :, pl.ds(pl.multiple_of(at * points, points), points)] = val_wide[
                pl.ds(at * group + copy * own, own), :
            ].astype(narrow)
        return carry

    lax.fori_loop(0, seqs, pack_part, 0, unroll=4)
    part_copies = []
    for step in range(1, copies):
        there = lax.rem(mine + step, copies)
        part_copies.append(near(2, step, part_out.at[there], part_in.at[mine]))
        part_copies.append(near(3, step, gain_out.at[there], gain_in.at[mine]))
    for copy in part_copies:
        copy.start()
    part_in[pl.ds(mine, 1)] = part_out[pl.ds(mine, 1)]
    gain_in[pl.ds(mine, 1)] = gain_out[pl.ds(mine, 1)]

    all_of(grad_out, grad_in, 2).wait_recv()

    def place(at, carry):
        block = grad_in[pl.ds(at * per_tile, per_tile)].reshape(lanes, points)
        grad_ref[:, pl.ds(pl.multiple_of(at * lanes, lanes), lanes)] = block.T
        return carry

    lax.fori_loop(0, seqs // per_tile, place, 0, unroll=2)

    for copy in part_copies:
        copy.wait_recv()

    def sum_parts(at, carry):
        where = pl.ds(pl.multiple_of(at * points, points), points)
        total = part_in[0, :, where].astype(wide)
        for copy in range(1, copies):
            total = total + part_in[copy, :, where].astype(wide)
        grad_filter_ref[:, where] = total * scale
        return carry

    lax.fori_loop(0, seqs, sum_parts, 0, unroll=4)
    total = gain_in[0]
    for copy in range(1, copies):
        total = total + gain_in[copy]
    grad_gain_ref[...] = jnp.broadcast_to(jnp.sum(total, axis=1, keepdims=True) * scale, grad_gain_ref.shape)

    for copy in filter_copies + part_copies:
        copy.wait_send()
    all_of(cot_out, cot_in, 0).wait_send()
    all_of(val_out, val_in, 1).wait_send()
    all_of(grad_out, grad_in, 2).wait_send()


def shards(values, cotangent, long_filter, bypass):
    seqs, copies = lax.axis_size("seq"), lax.axis_size("dp")
    points, channels = values.shape[1:]
    group = channels // seqs
    own, length = long_filter.shape
    scale = 1.0 / math.sqrt(copies * length)
    consts = tables(seqs, points)
    gain = jnp.broadcast_to(bypass.astype(wide)[:, None], (own, lanes))
    vmem = pl.BlockSpec(memory_space=pltpu.VMEM)
    rows = pltpu.VMEM((seqs, group, points), narrow)
    grad, grad_filter, grad_gain = pl.pallas_call(
        functools.partial(kernel, seqs, copies, scale),
        out_shape=(
            jax.ShapeDtypeStruct((points, channels), narrow),
            jax.ShapeDtypeStruct((own, length), wide),
            jax.ShapeDtypeStruct((own, lanes), wide),
        ),
        in_specs=[vmem] * 9,
        out_specs=(vmem,) * 3,
        scratch_shapes=[
            rows,
            rows,
            rows,
            rows,
            pltpu.VMEM((copies, own, length), narrow),
            pltpu.VMEM((copies, own, lanes), wide),
            pltpu.VMEM((seqs * group, points), wide),
            pltpu.VMEM((seqs * group, points), wide),
            pltpu.VMEM((group, seqs, 2 * points), narrow),
            pltpu.VMEM((group, seqs, 2 * points), narrow),
            rows,
            rows,
            pltpu.VMEM((copies, own, length), narrow),
            pltpu.VMEM((copies, own, length), narrow),
            pltpu.VMEM((copies, own, lanes), wide),
            pltpu.VMEM((copies, own, lanes), wide),
            pltpu.SemaphoreType.DMA((3,)),
            pltpu.SemaphoreType.DMA((3,)),
            pltpu.SemaphoreType.DMA((4, copies)),
            pltpu.SemaphoreType.DMA((4, copies)),
        ],
        compiler_params=pltpu.CompilerParams(
            collective_id=0, has_side_effects=True, vmem_limit_bytes=48 * 1024 * 1024
        ),
    )(values[0], cotangent[0], long_filter, gain, *consts)
    return grad[None], grad_filter, grad_gain[:, 0]


def solution(mesh):
    placed = (P("dp", "seq", None), P("dp", "seq", None), P(("seq", "dp"), None), P(("seq", "dp")))
    return jax.shard_map(
        shards,
        mesh=mesh,
        in_specs=placed,
        out_specs=(P("dp", "seq", None), P(("seq", "dp"), None), P(("seq", "dp"))),
        check_vma=False,
    )
```

time: 520 us -> 123 us (0.24); the launches traced: 510 us -> 122 us
  other arithmetic: 175 us -> 0 us
  local copies, waits for them, and re-layouts: 159 us -> 10.9 us
  Pallas kernels: 0 us -> 111 us
  starting transfers between devices: 75.9 us -> 0 us
  matrix products: 64.8 us -> 0 us
  waiting for transfers between devices: 33.9 us -> 0 us
    unnamed x7 -> x0, other arithmetic: 154 us -> none
    pallas_call x0 -> x1, Pallas kernels: none -> 111 us  [shards(): pl.pallas_call(functools.partial(kernel, seqs, copies, scale), out_shape=...]
    all_to_all x6 -> x0, starting transfers between devices: 75.9 us -> none  [the longest x1 25.5 us: shards(): lax.all_to_all(grad_rows, 'seq', split_axis=2, concat_axis=1, tiled=True)]
    unnamed x84 -> x20, local copies, waits for them, and re-layouts: 76.5 us -> 10.2 us
    dot_general x30 -> x0, matrix products: 64.8 us -> none  [contract(): return jnp.einsum(form, table, data, preferred_element_type=jnp.float32)]
    all_to_all x10 -> x0, local copies, waits for them, and re-layouts: 56.1 us -> none  [the longest x1 16 us: shards(): lax.all_to_all(grad_rows, 'dp', split_axis=0, concat_axis=1, tiled=True)]
    all_to_all x6 -> x0, waiting for transfers between devices: 33.9 us -> none  [the longest x1 28.3 us: shards(): lax.all_to_all(grad_rows, 'seq', split_axis=2, concat_axis=1, tiled=True)]
    reshape x5 -> x0, local copies, waits for them, and re-layouts: 20.1 us -> none  [the longest x2 8.5 us: forward_padded(): out_real.reshape(leading + (points,))]
  transfers between devices with their start and end apart: 6 -> 0, of which waited for: 3 -> 0; matrix products, arithmetic and copies ran while one was open for 22% -> 0% of each run, Pallas kernels for 0% -> 0%
where the time goes in v1:
time: 123 us; the launch traced here: 122 us
  Pallas kernels  111 us (90%)
  local copies, waits for them, and re-layouts  10.9 us (9%)
    pallas_call x1, Pallas kernels, shards(): pl.pallas_call(functools.partial(kernel, seqs, copies, scale), out_shape=...  111 us
    unnamed x20, local copies, waits for them, and re-layouts  10.2 us

profile of v1, /device:TPU:1, one launch (start us, length us, event | category | flops | bytes accessed | tf_op | source)
XLA Modules:
  0.0 122.3 jit_solution(10888652952596591241)
XLA Ops:
  0.6 0.0 copy-start.8
  0.6 0.6 copy-done.8
  1.3 0.1 broadcast_in_dim.4.gain_ref
  1.4 0.0 copy-start
  1.4 1.2 copy-done
  2.6 0.0 copy-start.1
  2.6 1.2 copy-done.1
  3.8 0.0 copy-start.2
  3.8 0.9 copy-done.2
  4.8 0.0 copy-start.3
  4.8 0.9 copy-done.3
  5.7 0.0 copy-start.4
  5.7 0.9 copy-done.4
  6.6 0.0 copy-start.5
  6.6 0.9 copy-done.5
  7.5 0.0 copy-start.6
  7.5 0.8 copy-done.6
  8.3 0.0 copy-start.7
  8.3 0.8 copy-done.7
  9.2 110.8 %shard_map.112 = (bf16[128,4096]{1,0:T(8,128)(2,1)S(1)}, f32[8,16384]{1,0:T(8,128)S(1)}, f32[8,128]{1,0:T(8,128)S(1)}) custom-call(bf16[128,4096]{1,0:T(8,128)(2,1)S(1)} %bitcast.3, bf16[128,4096]{1,0:T(8,128)(2,1)S(1)} %bitcast.4, bf16[8,16384]{1,0:T(8,128)(2,1)S(1)} %copy-done.2, f32[8,128]{1,0:T(8,128)S(1)} %broadcast_in_dim.4.gain_ref, ...), custom_call_target="tpu_custom_call" | custom-call | tf_op jit(solution)/shard_map/pallas_call | solution.py:296
  119.9 0.6 slice_reduce_fusion
  120.6 1.0 copy.14
  121.5 0.8 copy.15
Async XLA Ops:
  0.6 0.7 copy-start.8
  1.4 1.2 %copy-start = (bf16[1,128,4096]{2,1,0:T(8,128)(2,1)S(1)}, bf16[1,128,4096]{2,1,0:T(8,128)(2,1)}, u32[]{:S(2)}) copy-start(bf16[1,128,4096]{2,1,0:T(8,128)(2,1)} %param.9) | copy-start | bytes 3145732
  2.6 1.2 %copy-start.1 = (bf16[1,128,4096]{2,1,0:T(8,128)(2,1)S(1)}, bf16[1,128,4096]{2,1,0:T(8,128)(2,1)}, u32[]{:S(2)}) copy-start(bf16[1,128,4096]{2,1,0:T(8,128)(2,1)} %param.10) | copy-start | bytes 3145732
  3.8 0.9 copy-start.2
  4.8 0.9 copy-start.3
  5.7 0.9 copy-start.4
  6.6 0.9 copy-start.5
  7.5 0.8 copy-start.6
  8.3 0.8 copy-start.7

commit v2 on v1

--- a/solution.py
+++ b/solution.py
@@ -34,25 +34,62 @@
 
 
 def kernel(
-    seqs, copies, scale,
+    seqs, copies, cuts, scale,
+    values_hbm, cotangent_hbm, filter_hbm, gain_hbm, outer_hbm, inner_hbm, back_inner_hbm, back_outer_hbm, turn_hbm,
+    grad_ref, grad_filter_ref, grad_gain_ref,
     values_ref, cotangent_ref, filter_ref, gain_ref, outer_ref, inner_ref, back_inner_ref, back_outer_ref, turn_ref,
-    grad_ref, grad_filter_ref, grad_gain_ref,
     cot_out, val_out, cot_in, val_in, filters, gains, cot_wide, val_wide, cot_spec, filter_spec,
-    grad_out, grad_in, part_out, part_in, gain_out, gain_in, send_sem, recv_sem, near_send_sem, near_recv_sem,
+    grad_out, grad_in, part_out, part_in, gain_out, gain_in,
+    load_sem, send_sem, recv_sem, near_send_sem, near_recv_sem, ready_sem,
 ):
     me, mine = lax.axis_index("seq"), lax.axis_index("dp")
     points = values_ref.shape[0]
     group = cot_in.shape[1]
     own = filter_ref.shape[0]
     per_tile = lanes // group
+    width = group // cuts
+    shares = copies // cuts
+    plane = 1 << (seqs.bit_length() // 2)
+    columns = seqs // plane
+
+    loads = {}
+    for at, (name, src_ref, dst_ref) in enumerate(
+        (
+            ("cotangent", cotangent_hbm, cotangent_ref),
+            ("filter", filter_hbm, filter_ref),
+            ("gain", gain_hbm, gain_ref),
+            ("values", values_hbm, values_ref),
+            ("outer", outer_hbm, outer_ref),
+            ("inner", inner_hbm, inner_ref),
+            ("turn", turn_hbm, turn_ref),
+            ("back_inner", back_inner_hbm, back_inner_ref),
+            ("back_outer", back_outer_hbm, back_outer_ref),
+        )
+    ):
+        loads[name] = pltpu.make_async_copy(src_ref, dst_ref, load_sem.at[at])
+        loads[name].start()
 
     barrier = pltpu.get_barrier_semaphore()
-
-    def greet(step, carry):
-        pl.semaphore_signal(barrier, inc=1, device_id={"seq": lax.rem(me + step, seqs)}, device_id_type=MESH)
-        return carry
-
-    lax.fori_loop(1, seqs, greet, 0)
+    in_plane, in_column = lax.rem(me, plane), me // plane
+
+    def column_peer(step):
+        return lax.rem(in_column + step, columns) * plane + in_plane
+
+    def greet_column(step, carry):
+        pl.semaphore_signal(barrier, inc=1, device_id={"seq": column_peer(step)}, device_id_type=MESH)
+        return carry
+
+    def greet_plane(step, carry):
+        peer = in_column * plane + lax.rem(in_plane + step, plane)
+        pl.semaphore_signal(barrier, inc=1, device_id={"seq": peer}, device_id_type=MESH)
+        return carry
+
+    def tell_column(step, carry):
+        pl.semaphore_signal(ready_sem, inc=1, device_id={"seq": column_peer(step)}, device_id_type=MESH)
+        return carry
+
+    lax.fori_loop(1, columns, greet_column, 0)
+    lax.fori_loop(1, plane, greet_plane, 0)
     for step in range(1, copies):
         pl.semaphore_signal(barrier, inc=1, device_id={"dp": lax.rem(mine + step, copies)}, device_id_type=MESH)
 
@@ -64,28 +101,31 @@
 
         lax.fori_loop(0, seqs // per_tile, tile, 0, unroll=2)
 
-    def send(rows_ref, there_ref, which):
+    def send(rows_ref, there_ref, which, cut):
+        part = pl.ds(cut * width, width)
+
         def one(step, carry):
             peer = lax.rem(me + step * 17, seqs)
             pltpu.make_async_remote_copy(
-                src_ref=rows_ref.at[peer],
-                dst_ref=there_ref.at[me],
-                send_sem=send_sem.at[which],
-                recv_sem=recv_sem.at[which],
+                src_ref=rows_ref.at[peer, part],
+                dst_ref=there_ref.at[me, part],
+                send_sem=send_sem.at[which, cut],
+                recv_sem=recv_sem.at[which, cut],
                 device_id={"seq": peer},
                 device_id_type=MESH,
             ).start()
             return carry
 
         lax.fori_loop(1, seqs, one, 0)
-        there_ref[pl.ds(me, 1)] = rows_ref[pl.ds(me, 1)]
-
-    def all_of(rows_ref, there_ref, which):
+        there_ref[pl.ds(me, 1), part] = rows_ref[pl.ds(me, 1), part]
+
+    def all_of(rows_ref, there_ref, which, cut):
+        part = pl.ds(cut * width, width)
         return pltpu.make_async_remote_copy(
-            src_ref=rows_ref.at[pl.ds(0, seqs - 1)],
-            dst_ref=there_ref.at[pl.ds(0, seqs - 1)],
-            send_sem=send_sem.at[which],
-            recv_sem=recv_sem.at[which],
+            src_ref=rows_ref.at[pl.ds(0, seqs - 1), part],
+            dst_ref=there_ref.at[pl.ds(0, seqs - 1), part],
+            send_sem=send_sem.at[which, cut],
+            recv_sem=recv_sem.at[which, cut],
             device_id={"seq": lax.rem(me + 1, seqs)},
             device_id_type=MESH,
         )
@@ -100,21 +140,32 @@
             device_id_type=MESH,
         )
 
+    pl.semaphore_wait(barrier, plane + columns + copies - 3)
+    lax.fori_loop(1, columns, tell_column, 0)
+    loads["cotangent"].wait()
     turn_round(cotangent_ref, cot_out)
-    pl.semaphore_wait(barrier, seqs + copies - 2)
+    loads["filter"].wait()
+    loads["gain"].wait()
+    filters[pl.ds(mine, 1)] = filter_ref[...][None]
+    gains[pl.ds(mine, 1)] = gain_ref[...][None]
+    pl.semaphore_wait(ready_sem, columns - 1)
 
     filter_copies = []
     for step in range(1, copies):
         filter_copies.append(near(0, step, filter_ref, filters.at[mine]))
         filter_copies.append(near(1, step, gain_ref, gains.at[mine]))
+    send(cot_out, cot_in, 0, 0)
     for copy in filter_copies:
         copy.start()
-    filters[pl.ds(mine, 1)] = filter_ref[...][None]
-    gains[pl.ds(mine, 1)] = gain_ref[...][None]
-    send(cot_out, cot_in, 0)
+    loads["values"].wait()
     turn_round(values_ref, val_out)
-    send(val_out, val_in, 1)
-
+    send(val_out, val_in, 1, 0)
+    for cut in range(1, cuts):
+        send(cot_out, cot_in, 0, cut)
+        send(val_out, val_in, 1, cut)
+
+    for name in ("outer", "inner", "turn", "back_inner", "back_outer"):
+        loads[name].wait()
     outer, inner = outer_ref[...], inner_ref[...]
     back_inner, back_outer = back_inner_ref[...], back_outer_ref[...]
     dot = functools.partial(jnp.dot, preferred_element_type=wide)
@@ -176,15 +227,7 @@
             filter_spec[at + offset] = specs[offset].astype(narrow)
         return carry
 
-    lax.fori_loop(0, group // 2, filter_pair, 0)
-
-    all_of(cot_out, cot_in, 0).wait_recv()
-
-    def widen_cot(at, carry):
-        cot_wide[pl.ds(pl.multiple_of(at * group, group), group), :] = cot_in[at].astype(wide)
-        return carry
-
-    lax.fori_loop(0, seqs, widen_cot, 0, unroll=4)
+    lax.fori_loop(0, group // 2, filter_pair, 0, unroll=2)
 
     def grad_pair(pair, carry):
         at = pair * 2
@@ -202,25 +245,6 @@
             cot_wide[pl.ds(channel, seqs, stride=group), :] = signals[offset] + gain * rows[offset]
         return carry
 
-    lax.fori_loop(0, group // 2, grad_pair, 0)
-
-    def pack_grad(at, carry):
-        grad_out[at] = cot_wide[pl.ds(pl.multiple_of(at * group, group), group), :].astype(narrow)
-        return carry
-
-    lax.fori_loop(0, seqs, pack_grad, 0, unroll=4)
-    send(grad_out, grad_in, 2)
-
-    all_of(val_out, val_in, 1).wait_recv()
-
-    def widen_val(at, total):
-        block = val_in[at].astype(wide)
-        val_wide[pl.ds(pl.multiple_of(at * group, group), group), :] = block
-        return total + block * cot_in[at].astype(wide)
-
-    total = lax.fori_loop(0, seqs, widen_val, jnp.zeros((group, points), wide), unroll=4)
-    gain_out[...] = total.reshape(copies, own, points)
-
     def cross_pair(pair, carry):
         at = pair * 2
         specs = transform(rows_of(val_wide, at), rows_of(val_wide, at + 1))
@@ -230,36 +254,69 @@
             val_wide[pl.ds(at + offset, seqs, stride=group), :] = signals[offset]
         return carry
 
-    lax.fori_loop(0, group // 2, cross_pair, 0)
-
-    def pack_part(at, carry):
-        for copy in range(copies):
-            part_out[copy, :, pl.ds(pl.multiple_of(at * points, points), points)] = val_wide[
-                pl.ds(at * group + copy * own, own), :
-            ].astype(narrow)
-        return carry
-
-    lax.fori_loop(0, seqs, pack_part, 0, unroll=4)
-    part_copies = []
+    part_copies, gain_copies = [], []
     for step in range(1, copies):
         there = lax.rem(mine + step, copies)
-        part_copies.append(near(2, step, part_out.at[there], part_in.at[mine]))
-        part_copies.append(near(3, step, gain_out.at[there], gain_in.at[mine]))
-    for copy in part_copies:
-        copy.start()
+        part_copies.append((there, near(2, step, part_out.at[there], part_in.at[mine])))
+        gain_copies.append((there, near(3, step, gain_out.at[there], gain_in.at[mine])))
+
+    for cut in range(cuts):
+        part = pl.ds(cut * width, width)
+
+        def rows_at(at):
+            return pl.ds(pl.multiple_of(at * group + cut * width, width), width)
+
+        all_of(cot_out, cot_in, 0, cut).wait_recv()
+
+        def widen_cot(at, carry):
+            cot_wide[rows_at(at), :] = cot_in[at, part].astype(wide)
+            return carry
+
+        lax.fori_loop(0, seqs, widen_cot, 0, unroll=4)
+        lax.fori_loop(cut * width // 2, (cut + 1) * width // 2, grad_pair, 0, unroll=2)
+
+        def pack_grad(at, carry):
+            grad_out[at, part] = cot_wide[rows_at(at), :].astype(narrow)
+            return carry
+
+        lax.fori_loop(0, seqs, pack_grad, 0, unroll=4)
+        send(grad_out, grad_in, 2, cut)
+
+        all_of(val_out, val_in, 1, cut).wait_recv()
+
+        def widen_val(at, total):
+            block = val_in[at, part].astype(wide)
+            val_wide[rows_at(at), :] = block
+            return total + block * cot_in[at, part].astype(wide)
+
+        total = lax.fori_loop(0, seqs, widen_val, jnp.zeros((width, points), wide), unroll=4)
+        gain_out[pl.ds(cut * shares, shares)] = total.reshape(shares, own, points)
+        lax.fori_loop(cut * width // 2, (cut + 1) * width // 2, cross_pair, 0, unroll=2)
+
+        def pack_part(at, carry):
+            for copy in range(cut * shares, (cut + 1) * shares):
+                part_out[copy, :, pl.ds(pl.multiple_of(at * points, points), points)] = val_wide[
+                    pl.ds(at * group + copy * own, own), :
+                ].astype(narrow)
+            return carry
+
+        lax.fori_loop(0, seqs, pack_part, 0, unroll=4)
+        for there, copy in part_copies + gain_copies:
+            pl.when(there // shares == cut)(copy.start)
+
     part_in[pl.ds(mine, 1)] = part_out[pl.ds(mine, 1)]
     gain_in[pl.ds(mine, 1)] = gain_out[pl.ds(mine, 1)]
-
-    all_of(grad_out, grad_in, 2).wait_recv()
 
     def place(at, carry):
         block = grad_in[pl.ds(at * per_tile, per_tile)].reshape(lanes, points)
         grad_ref[:, pl.ds(pl.multiple_of(at * lanes, lanes), lanes)] = block.T
         return carry
 
+    for cut in range(cuts):
+        all_of(grad_out, grad_in, 2, cut).wait_recv()
     lax.fori_loop(0, seqs // per_tile, place, 0, unroll=2)
 
-    for copy in part_copies:
+    for there, copy in part_copies + gain_copies:
         copy.wait_recv()
 
     def sum_parts(at, carry):
@@ -276,11 +333,14 @@
         total = total + gain_in[copy]
     grad_gain_ref[...] = jnp.broadcast_to(jnp.sum(total, axis=1, keepdims=True) * scale, grad_gain_ref.shape)
 
-    for copy in filter_copies + part_copies:
+    for copy in filter_copies:
         copy.wait_send()
-    all_of(cot_out, cot_in, 0).wait_send()
-    all_of(val_out, val_in, 1).wait_send()
-    all_of(grad_out, grad_in, 2).wait_send()
+    for there, copy in part_copies + gain_copies:
+        copy.wait_send()
+    for cut in range(cuts):
+        all_of(cot_out, cot_in, 0, cut).wait_send()
+        all_of(val_out, val_in, 1, cut).wait_send()
+        all_of(grad_out, grad_in, 2, cut).wait_send()
 
 
 def shards(values, cotangent, long_filter, bypass):
@@ -291,18 +351,21 @@
     scale = 1.0 / math.sqrt(copies * length)
     consts = tables(seqs, points)
     gain = jnp.broadcast_to(bypass.astype(wide)[:, None], (own, lanes))
-    vmem = pl.BlockSpec(memory_space=pltpu.VMEM)
+    vmem, hbm = pl.BlockSpec(memory_space=pltpu.VMEM), pl.BlockSpec(memory_space=pltpu.HBM)
+    operands = (values[0], cotangent[0], long_filter, gain, *consts)
+    cuts = 2
     rows = pltpu.VMEM((seqs, group, points), narrow)
     grad, grad_filter, grad_gain = pl.pallas_call(
-        functools.partial(kernel, seqs, copies, scale),
+        functools.partial(kernel, seqs, copies, cuts, scale),
         out_shape=(
             jax.ShapeDtypeStruct((points, channels), narrow),
             jax.ShapeDtypeStruct((own, length), wide),
             jax.ShapeDtypeStruct((own, lanes), wide),
         ),
-        in_specs=[vmem] * 9,
+        in_specs=[hbm] * len(operands),
         out_specs=(vmem,) * 3,
         scratch_shapes=[
+            *[pltpu.VMEM(operand.shape, operand.dtype) for operand in operands],
             rows,
             rows,
             rows,
@@ -319,15 +382,17 @@
             pltpu.VMEM((copies, own, length), narrow),
             pltpu.VMEM((copies, own, lanes), wide),
             pltpu.VMEM((copies, own, lanes), wide),
-            pltpu.SemaphoreType.DMA((3,)),
-            pltpu.SemaphoreType.DMA((3,)),
+            pltpu.SemaphoreType.DMA((len(operands),)),
+            pltpu.SemaphoreType.DMA((3, cuts)),
+            pltpu.SemaphoreType.DMA((3, cuts)),
             pltpu.SemaphoreType.DMA((4, copies)),
             pltpu.SemaphoreType.DMA((4, copies)),
+            pltpu.SemaphoreType.REGULAR,
         ],
         compiler_params=pltpu.CompilerParams(
             collective_id=0, has_side_effects=True, vmem_limit_bytes=48 * 1024 * 1024
         ),
-    )(values[0], cotangent[0], long_filter, gain, *consts)
+    )(*operands)
     return grad[None], grad_filter, grad_gain[:, 0]
 
 

time: 123 us -> 114 us (0.927)
  Pallas kernels: 111 us -> 101 us
    pallas_call x1, Pallas kernels: 111 us -> 101 us  [shards(): pl.pallas_call(functools.partial(kernel, seqs, copies, cuts, scale), out_...]
where the time goes in v2:
time: 114 us; the launch traced here: 112 us
  Pallas kernels  101 us (89%)
  local copies, waits for them, and re-layouts  10.9 us (10%)
    pallas_call x1, Pallas kernels, shards(): pl.pallas_call(functools.partial(kernel, seqs, copies, cuts, scale), out_...  101 us
    unnamed x20, local copies, waits for them, and re-layouts  10.2 us

profile of v2, /device:TPU:1, one launch (start us, length us, event | category | flops | bytes accessed | tf_op | source)
XLA Modules:
  0.0 112.4 jit_solution(4208556438777112527)
XLA Ops:
  0.6 0.0 copy-start.8
  0.6 0.6 copy-done.8
  1.3 0.1 broadcast_in_dim.4.gain_hbm
  1.4 0.0 copy-start
  1.4 1.2 %copy-done = bf16[1,128,4096]{2,1,0:T(8,128)(2,1)S(1)} copy-done((bf16[1,128,4096]{2,1,0:T(8,128)(2,1)S(1)}, bf16[1,128,4096]{2,1,0:T(8,128)(2,1)}, u32[]{:S(2)}) %copy-start) | copy-done | bytes 1048600
  2.6 0.0 copy-start.1
  2.6 1.2 %copy-done.1 = bf16[1,128,4096]{2,1,0:T(8,128)(2,1)S(1)} copy-done((bf16[1,128,4096]{2,1,0:T(8,128)(2,1)S(1)}, bf16[1,128,4096]{2,1,0:T(8,128)(2,1)}, u32[]{:S(2)}) %copy-start.1) | copy-done | bytes 1048600
  3.8 0.0 copy-start.2
  3.8 0.9 copy-done.2
  4.8 0.0 copy-start.3
  4.8 0.9 copy-done.3
  5.7 0.0 copy-start.4
  5.7 0.9 copy-done.4
  6.6 0.0 copy-start.5
  6.6 0.9 copy-done.5
  7.5 0.0 copy-start.6
  7.5 0.8 copy-done.6
  8.3 0.0 copy-start.7
  8.3 0.8 copy-done.7
  9.2 100.8 %shard_map.112 = (bf16[128,4096]{1,0:T(8,128)(2,1)S(1)}, f32[8,16384]{1,0:T(8,128)S(1)}, f32[8,128]{1,0:T(8,128)S(1)}) custom-call(bf16[128,4096]{1,0:T(8,128)(2,1)S(1)} %bitcast.3, bf16[128,4096]{1,0:T(8,128)(2,1)S(1)} %bitcast.4, bf16[8,16384]{1,0:T(8,128)(2,1)S(1)} %copy-done.2, f32[8,128]{1,0:T(8,128)S(1)} %broadcast_in_dim.4.gain_hbm, ...), custom_call_target="tpu_custom_call" | custom-call | tf_op jit(solution)/shard_map/pallas_call | solution.py:358
  110.0 0.6 slice_reduce_fusion
  110.6 1.0 copy.14
  111.6 0.8 copy.15
Async XLA Ops:
  0.6 0.7 copy-start.8
  1.4 1.2 %copy-start = (bf16[1,128,4096]{2,1,0:T(8,128)(2,1)S(1)}, bf16[1,128,4096]{2,1,0:T(8,128)(2,1)}, u32[]{:S(2)}) copy-start(bf16[1,128,4096]{2,1,0:T(8,128)(2,1)} %param.9) | copy-start | bytes 3145732
  2.6 1.2 %copy-start.1 = (bf16[1,128,4096]{2,1,0:T(8,128)(2,1)S(1)}, bf16[1,128,4096]{2,1,0:T(8,128)(2,1)}, u32[]{:S(2)}) copy-start(bf16[1,128,4096]{2,1,0:T(8,128)(2,1)} %param.10) | copy-start | bytes 3145732
  3.8 0.9 copy-start.2
  4.8 0.9 copy-start.3
  5.7 0.9 copy-start.4
  6.6 0.9 copy-start.5
  7.5 0.8 copy-start.6
  8.3 0.8 copy-start.7

commit v3 on v2

--- a/solution.py
+++ b/solution.py
@@ -39,7 +39,7 @@
     grad_ref, grad_filter_ref, grad_gain_ref,
     values_ref, cotangent_ref, filter_ref, gain_ref, outer_ref, inner_ref, back_inner_ref, back_outer_ref, turn_ref,
     cot_out, val_out, cot_in, val_in, filters, gains, cot_wide, val_wide, cot_spec, filter_spec,
-    grad_out, grad_in, part_out, part_in, gain_out, gain_in,
+    grad_out, grad_in, part_out, part_in, passed_in, gain_out, gain_in,
     load_sem, send_sem, recv_sem, near_send_sem, near_recv_sem, ready_sem,
 ):
     me, mine = lax.axis_index("seq"), lax.axis_index("dp")
@@ -51,6 +51,15 @@
     shares = copies // cuts
     plane = 1 << (seqs.bit_length() // 2)
     columns = seqs // plane
+    half = filter_ref.shape[1] // 2
+    right, left = 1, copies - 1
+    first = 1 - mine // shares
+
+    def rows_of_cut(cut):
+        return pl.ds(pl.multiple_of(lax.rem(first + cut, cuts) * width, width), width)
+
+    def dp_at(step):
+        return lax.rem(mine + step, copies)
 
     loads = {}
     for at, (name, src_ref, dst_ref) in enumerate(
@@ -102,7 +111,7 @@
         lax.fori_loop(0, seqs // per_tile, tile, 0, unroll=2)
 
     def send(rows_ref, there_ref, which, cut):
-        part = pl.ds(cut * width, width)
+        part = rows_of_cut(cut)
 
         def one(step, carry):
             peer = lax.rem(me + step * 17, seqs)
@@ -120,7 +129,7 @@
         there_ref[pl.ds(me, 1), part] = rows_ref[pl.ds(me, 1), part]
 
     def all_of(rows_ref, there_ref, which, cut):
-        part = pl.ds(cut * width, width)
+        part = rows_of_cut(cut)
         return pltpu.make_async_remote_copy(
             src_ref=rows_ref.at[pl.ds(0, seqs - 1), part],
             dst_ref=there_ref.at[pl.ds(0, seqs - 1), part],
@@ -150,16 +159,21 @@
     gains[pl.ds(mine, 1)] = gain_ref[...][None]
     pl.semaphore_wait(ready_sem, columns - 1)
 
-    filter_copies = []
-    for step in range(1, copies):
-        filter_copies.append(near(0, step, filter_ref, filters.at[mine]))
-        filter_copies.append(near(1, step, gain_ref, gains.at[mine]))
+    filter_copies = [near(0, step, filter_ref, filters.at[mine]) for step in (right, left)]
+    gain_copies = [near(1, step, gain_ref, gains.at[mine]) for step in range(1, copies)]
+    filter_passes = []
+    for step, start in ((right, 0), (left, half)):
+        passed = filters.at[dp_at(copies - step), :, pl.ds(start, half)]
+        filter_passes.append(near(4, step, passed, passed))
     send(cot_out, cot_in, 0, 0)
-    for copy in filter_copies:
+    for copy in filter_copies + gain_copies:
         copy.start()
     loads["values"].wait()
     turn_round(values_ref, val_out)
     send(val_out, val_in, 1, 0)
+    for copy, onward in zip(filter_copies, filter_passes):
+        copy.wait_recv()
+        onward.start()
     for cut in range(1, cuts):
         send(cot_out, cot_in, 0, cut)
         send(val_out, val_in, 1, cut)
@@ -208,7 +222,7 @@
         both = dot(back_outer, jnp.concatenate(turned, 1))
         return both[:, :points], both[:, points:]
 
-    for copy in filter_copies:
+    for copy in filter_passes + gain_copies:
         copy.wait_recv()
 
     def widen_filter(at, carry):
@@ -254,17 +268,37 @@
             val_wide[pl.ds(at + offset, seqs, stride=group), :] = signals[offset]
         return carry
 
-    part_copies, gain_copies = [], []
-    for step in range(1, copies):
-        there = lax.rem(mine + step, copies)
-        part_copies.append((there, near(2, step, part_out.at[there], part_in.at[mine])))
-        gain_copies.append((there, near(3, step, gain_out.at[there], gain_in.at[mine])))
+    part_copies = {}
+    pass_copies = []
+    for step, start in ((right, 0), (left, half)):
+        side = 0 if step == right else 1
+        part_copies[step] = near(2, step, part_out.at[dp_at(step)], part_in.at[side])
+        pass_copies.append(near(5, step, part_out.at[dp_at(2), :, pl.ds(start, half)], passed_in.at[side]))
+    gain_sums = [near(3, step, gain_out.at[dp_at(step)], gain_in.at[mine]) for step in range(1, copies)]
+
+    def hand_over(step):
+        side = 0 if step == right else 1
+        there = dp_at(step)
+        pass_copies[side].wait_recv()
+
+        def add(at, carry):
+            here = pl.multiple_of(at * points, points)
+            where = pl.ds(side * half + here, points)
+            sent_on = part_out[there, :, where].astype(wide) + passed_in[side, :, pl.ds(here, points)].astype(wide)
+            part_out[there, :, where] = sent_on.astype(narrow)
+            return carry
+
+        lax.fori_loop(0, seqs // 2, add, 0, unroll=min(4, seqs // 2))
+        part_copies[step].start()
+
+    even = lax.rem(mine, 2) == 0
 
     for cut in range(cuts):
-        part = pl.ds(cut * width, width)
+        part = rows_of_cut(cut)
+        begin = lax.rem(first + cut, cuts)
 
         def rows_at(at):
-            return pl.ds(pl.multiple_of(at * group + cut * width, width), width)
+            return pl.ds(pl.multiple_of(at * group + begin * width, width), width)
 
         all_of(cot_out, cot_in, 0, cut).wait_recv()
 
@@ -273,7 +307,7 @@
             return carry
 
         lax.fori_loop(0, seqs, widen_cot, 0, unroll=4)
-        lax.fori_loop(cut * width // 2, (cut + 1) * width // 2, grad_pair, 0, unroll=2)
+        lax.fori_loop(0, width // 2, lambda pair, carry: grad_pair(begin * (width // 2) + pair, carry), 0, unroll=2)
 
         def pack_grad(at, carry):
             grad_out[at, part] = cot_wide[rows_at(at), :].astype(narrow)
@@ -282,6 +316,9 @@
         lax.fori_loop(0, seqs, pack_grad, 0, unroll=4)
         send(grad_out, grad_in, 2, cut)
 
+        if cut == 1:
+            pl.when(even)(lambda: hand_over(left))
+            pl.when(jnp.logical_not(even))(lambda: hand_over(right))
         all_of(val_out, val_in, 1, cut).wait_recv()
 
         def widen_val(at, total):
@@ -290,21 +327,26 @@
             return total + block * cot_in[at, part].astype(wide)
 
         total = lax.fori_loop(0, seqs, widen_val, jnp.zeros((width, points), wide), unroll=4)
-        gain_out[pl.ds(cut * shares, shares)] = total.reshape(shares, own, points)
-        lax.fori_loop(cut * width // 2, (cut + 1) * width // 2, cross_pair, 0, unroll=2)
+        gain_out[pl.ds(begin * shares, shares)] = total.reshape(shares, own, points)
+        lax.fori_loop(0, width // 2, lambda pair, carry: cross_pair(begin * (width // 2) + pair, carry), 0, unroll=2)
 
         def pack_part(at, carry):
-            for copy in range(cut * shares, (cut + 1) * shares):
+            for share in range(shares):
+                copy = begin * shares + share
                 part_out[copy, :, pl.ds(pl.multiple_of(at * points, points), points)] = val_wide[
-                    pl.ds(at * group + copy * own, own), :
+                    pl.ds(pl.multiple_of(at * group + copy * own, own), own), :
                 ].astype(narrow)
             return carry
 
         lax.fori_loop(0, seqs, pack_part, 0, unroll=4)
-        for there, copy in part_copies + gain_copies:
-            pl.when(there // shares == cut)(copy.start)
-
-    part_in[pl.ds(mine, 1)] = part_out[pl.ds(mine, 1)]
+        if cut == 0:
+            for copy in pass_copies:
+                copy.start()
+        else:
+            pl.when(even)(lambda: hand_over(right))
+            pl.when(jnp.logical_not(even))(lambda: hand_over(left))
+    for copy in gain_sums:
+        copy.start()
     gain_in[pl.ds(mine, 1)] = gain_out[pl.ds(mine, 1)]
 
     def place(at, carry):
@@ -316,15 +358,13 @@
         all_of(grad_out, grad_in, 2, cut).wait_recv()
     lax.fori_loop(0, seqs // per_tile, place, 0, unroll=2)
 
-    for there, copy in part_copies + gain_copies:
+    for copy in [*part_copies.values(), *gain_sums]:
         copy.wait_recv()
 
     def sum_parts(at, carry):
         where = pl.ds(pl.multiple_of(at * points, points), points)
-        total = part_in[0, :, where].astype(wide)
-        for copy in range(1, copies):
-            total = total + part_in[copy, :, where].astype(wide)
-        grad_filter_ref[:, where] = total * scale
+        total = part_out[mine, :, where].astype(wide) + part_in[0, :, where].astype(wide)
+        grad_filter_ref[:, where] = (total + part_in[1, :, where].astype(wide)) * scale
         return carry
 
     lax.fori_loop(0, seqs, sum_parts, 0, unroll=4)
@@ -333,9 +373,7 @@
         total = total + gain_in[copy]
     grad_gain_ref[...] = jnp.broadcast_to(jnp.sum(total, axis=1, keepdims=True) * scale, grad_gain_ref.shape)
 
-    for copy in filter_copies:
-        copy.wait_send()
-    for there, copy in part_copies + gain_copies:
+    for copy in filter_copies + gain_copies + filter_passes + pass_copies + [*part_copies.values(), *gain_sums]:
         copy.wait_send()
     for cut in range(cuts):
         all_of(cot_out, cot_in, 0, cut).wait_send()
@@ -379,18 +417,19 @@
             rows,
             rows,
             pltpu.VMEM((copies, own, length), narrow),
-            pltpu.VMEM((copies, own, length), narrow),
+            pltpu.VMEM((2, own, length), narrow),
+            pltpu.VMEM((2, own, length // 2), narrow),
             pltpu.VMEM((copies, own, lanes), wide),
             pltpu.VMEM((copies, own, lanes), wide),
             pltpu.SemaphoreType.DMA((len(operands),)),
             pltpu.SemaphoreType.DMA((3, cuts)),
             pltpu.SemaphoreType.DMA((3, cuts)),
-            pltpu.SemaphoreType.DMA((4, copies)),
-            pltpu.SemaphoreType.DMA((4, copies)),
+            pltpu.SemaphoreType.DMA((6, copies)),
+            pltpu.SemaphoreType.DMA((6, copies)),
             pltpu.SemaphoreType.REGULAR,
         ],
         compiler_params=pltpu.CompilerParams(
-            collective_id=0, has_side_effects=True, vmem_limit_bytes=48 * 1024 * 1024
+            collective_id=0, has_side_effects=True, vmem_limit_bytes=64 * 1024 * 1024
         ),
     )(*operands)
     return grad[None], grad_filter, grad_gain[:, 0]

time: 114 us -> 105 us (0.921); the launches traced: 112 us -> 105 us
  local copies, waits for them, and re-layouts: 10.9 us -> 5.74 us
  Pallas kernels: 101 us -> 98.6 us
    unnamed x20 -> x8, local copies, waits for them, and re-layouts: 10.2 us -> 4.45 us
    pallas_call x1, Pallas kernels: 101 us -> 98.6 us  [shards(): pl.pallas_call(functools.partial(kernel, seqs, copies, cuts, scale), out_...]
where the time goes in v3:
time: 105 us
  Pallas kernels  98.6 us (94%)
  local copies, waits for them, and re-layouts  5.74 us (5%)
    pallas_call x1, Pallas kernels, shards(): pl.pallas_call(functools.partial(kernel, seqs, copies, cuts, scale), out_...  98.6 us
    unnamed x8, local copies, waits for them, and re-layouts  4.45 us

profile of v3, /device:TPU:1, one launch (start us, length us, event | category | flops | bytes accessed | tf_op | source)
XLA Modules:
  0.0 105.0 jit_solution(3106905399585533009)
XLA Ops:
  0.6 0.0 copy-start.2
  0.6 0.6 copy-done.2
  1.3 0.7 broadcast_in_dim.4.gain_hbm
  1.9 98.6 %shard_map.112 = (bf16[128,4096]{1,0:T(8,128)(2,1)}, f32[8,16384]{1,0:T(8,128)}, f32[8,128]{1,0:T(8,128)}) custom-call(bf16[128,4096]{1,0:T(8,128)(2,1)} %bitcast.3, bf16[128,4096]{1,0:T(8,128)(2,1)} %bitcast.4, bf16[8,16384]{1,0:T(8,128)(2,1)} %filter_hbm.1, f32[8,128]{1,0:T(8,128)} %broadcast_in_dim.4.gain_hbm, bf16[256,128]{1,0:T(8,128)(2,1)} %constant.10.clone.outer_hbm, ...), custom_call_target="tpu_custom_call" | custom-call | tf_op jit(solution)/shard_map/pallas_call | solution.py:396
  100.6 0.0 copy-start.1
  100.6 0.7 copy-done.1
  101.3 0.6 slice_reduce_fusion
  101.9 0.0 copy-start
  101.9 2.3 %copy.14 = bf16[1,128,4096]{2,1,0:T(8,128)(2,1)} copy(bf16[1,128,4096]{2,1,0:T(8,128)(2,1)} %bitcast.5) | data formatting | bytes 2097152
  104.2 0.0 copy-done
  104.2 0.8 copy.15
Async XLA Ops:
  0.6 0.7 copy-start.2
  100.6 0.7 copy-start.1
  101.9 2.3 %copy-start = (f32[8,16384]{1,0:T(8,128)S(1)}, f32[8,16384]{1,0:T(8,128)}, u32[]{:S(2)}) copy-start(f32[8,16384]{1,0:T(8,128)} %get-tuple-element.13) | copy-start | bytes 1572868

commit v4 on v3

--- a/solution.py
+++ b/solution.py
@@ -13,6 +13,7 @@
 MESH = pl.DeviceIdType.MESH
 lanes = 128
 wide = jnp.float32
+unroll = 4
 narrow = jnp.bfloat16
 
 
@@ -156,11 +157,13 @@
     loads["filter"].wait()
     loads["gain"].wait()
     filters[pl.ds(mine, 1)] = filter_ref[...][None]
-    gains[pl.ds(mine, 1)] = gain_ref[...][None]
+    diagonal = lax.broadcasted_iota(jnp.int32, (own, own), 0) == lax.broadcasted_iota(jnp.int32, (own, own), 1)
+    gain_square = jnp.where(diagonal, jnp.broadcast_to(gain_ref[...].astype(wide), (own, own)), 0.0)
+    gains[pl.ds(mine, 1)] = jnp.broadcast_to(jnp.sum(gain_square, axis=1, keepdims=True), (own, lanes))[None]
     pl.semaphore_wait(ready_sem, columns - 1)
 
     filter_copies = [near(0, step, filter_ref, filters.at[mine]) for step in (right, left)]
-    gain_copies = [near(1, step, gain_ref, gains.at[mine]) for step in range(1, copies)]
+    gain_copies = [near(1, step, gains.at[mine], gains.at[mine]) for step in range(1, copies)]
     filter_passes = []
     for step, start in ((right, 0), (left, half)):
         passed = filters.at[dp_at(copies - step), :, pl.ds(start, half)]
@@ -241,7 +244,7 @@
             filter_spec[at + offset] = specs[offset].astype(narrow)
         return carry
 
-    lax.fori_loop(0, group // 2, filter_pair, 0, unroll=2)
+    lax.fori_loop(0, group // 2, filter_pair, 0, unroll=unroll)
 
     def grad_pair(pair, carry):
         at = pair * 2
@@ -307,7 +310,7 @@
             return carry
 
         lax.fori_loop(0, seqs, widen_cot, 0, unroll=4)
-        lax.fori_loop(0, width // 2, lambda pair, carry: grad_pair(begin * (width // 2) + pair, carry), 0, unroll=2)
+        lax.fori_loop(0, width // 2, lambda pair, carry: grad_pair(begin * (width // 2) + pair, carry), 0, unroll=unroll)
 
         def pack_grad(at, carry):
             grad_out[at, part] = cot_wide[rows_at(at), :].astype(narrow)
@@ -328,7 +331,7 @@
 
         total = lax.fori_loop(0, seqs, widen_val, jnp.zeros((width, points), wide), unroll=4)
         gain_out[pl.ds(begin * shares, shares)] = total.reshape(shares, own, points)
-        lax.fori_loop(0, width // 2, lambda pair, carry: cross_pair(begin * (width // 2) + pair, carry), 0, unroll=2)
+        lax.fori_loop(0, width // 2, lambda pair, carry: cross_pair(begin * (width // 2) + pair, carry), 0, unroll=unroll)
 
         def pack_part(at, carry):
             for share in range(shares):
@@ -371,7 +374,8 @@
     total = gain_in[0]
     for copy in range(1, copies):
         total = total + gain_in[copy]
-    grad_gain_ref[...] = jnp.broadcast_to(jnp.sum(total, axis=1, keepdims=True) * scale, grad_gain_ref.shape)
+    total = jnp.broadcast_to(jnp.sum(total, axis=1, keepdims=True) * scale, (own, own))
+    grad_gain_ref[...] = jnp.sum(jnp.where(diagonal, total, 0.0), axis=0, keepdims=True)
 
     for copy in filter_copies + gain_copies + filter_passes + pass_copies + [*part_copies.values(), *gain_sums]:
         copy.wait_send()
@@ -388,17 +392,17 @@
     own, length = long_filter.shape
     scale = 1.0 / math.sqrt(copies * length)
     consts = tables(seqs, points)
-    gain = jnp.broadcast_to(bypass.astype(wide)[:, None], (own, lanes))
     vmem, hbm = pl.BlockSpec(memory_space=pltpu.VMEM), pl.BlockSpec(memory_space=pltpu.HBM)
-    operands = (values[0], cotangent[0], long_filter, gain, *consts)
+    operands = (values[0], cotangent[0], long_filter, bypass[None], *consts)
+    operands = [pltpu.with_memory_space_constraint(operand, pltpu.HBM) for operand in operands]
     cuts = 2
     rows = pltpu.VMEM((seqs, group, points), narrow)
     grad, grad_filter, grad_gain = pl.pallas_call(
         functools.partial(kernel, seqs, copies, cuts, scale),
         out_shape=(
-            jax.ShapeDtypeStruct((points, channels), narrow),
-            jax.ShapeDtypeStruct((own, length), wide),
-            jax.ShapeDtypeStruct((own, lanes), wide),
+            pltpu.VMEM((points, channels), narrow),
+            pltpu.VMEM((own, length), wide),
+            pltpu.VMEM((1, own), wide),
         ),
         in_specs=[hbm] * len(operands),
         out_specs=(vmem,) * 3,
@@ -429,10 +433,10 @@
             pltpu.SemaphoreType.REGULAR,
         ],
         compiler_params=pltpu.CompilerParams(
-            collective_id=0, has_side_effects=True, vmem_limit_bytes=64 * 1024 * 1024
+            collective_id=0, has_side_effects=True, vmem_limit_bytes=48 * 1024 * 1024
         ),
     )(*operands)
-    return grad[None], grad_filter, grad_gain[:, 0]
+    return grad[None], grad_filter, grad_gain[0]
 
 
 def solution(mesh):

time: 105 us -> 99.5 us (0.948)
  local copies, waits for them, and re-layouts: 5.74 us -> 2.28 us
  Pallas kernels: 98.6 us -> 96.5 us
    unnamed x8 -> x3, local copies, waits for them, and re-layouts: 4.45 us -> 2.28 us
    pallas_call x1, Pallas kernels: 98.6 us -> 96.5 us  [shards(): pl.pallas_call(functools.partial(kernel, seqs, copies, cuts, scale), out_...]
where the time goes in v4:
time: 99.5 us; the launch traced here: 99.4 us
  Pallas kernels  96.5 us (97%)
  local copies, waits for them, and re-layouts  2.28 us (2%)
    pallas_call x1, Pallas kernels, shards(): pl.pallas_call(functools.partial(kernel, seqs, copies, cuts, scale), out_...  96.5 us
    unnamed x3, local copies, waits for them, and re-layouts  2.28 us

profile of v4, /device:TPU:1, one launch (start us, length us, event | category | flops | bytes accessed | tf_op | source)
XLA Modules:
  0.0 99.4 jit_solution(15241928383857326317)
XLA Ops:
  0.6 96.5 %shard_map.112 = (bf16[128,4096]{1,0:T(8,128)(2,1)S(1)}, f32[8,16384]{1,0:T(8,128)S(1)}, f32[1,8]{1,0:T(1,128)S(1)}) custom-call(bf16[128,4096]{1,0:T(8,128)(2,1)} %bitcast.7, bf16[128,4096]{1,0:T(8,128)(2,1)} %bitcast.8, bf16[8,16384]{1,0:T(8,128)(2,1)} %filter_hbm.1, bf16[1,8]{1,0:T(2,128)(2,1)} %bitcast.9, bf16[256,128]{1,0:T(8,128)(2,1)} %constant.10.clone.outer_hbm, ...), custom_call_target="tpu_custom_call" | custom-call | tf_op jit(solution)/shard_map/pallas_call | solution.py:400
  97.1 1.0 copy.15
  98.1 0.5 copy.17
  98.6 0.8 copy.16

commit v5 on v4

--- a/solution.py
+++ b/solution.py
@@ -115,7 +115,7 @@
         part = rows_of_cut(cut)
 
         def one(step, carry):
-            peer = lax.rem(me + step * 17, seqs)
+            peer = lax.rem(me + step * 49, seqs)
             pltpu.make_async_remote_copy(
                 src_ref=rows_ref.at[peer, part],
                 dst_ref=there_ref.at[me, part],
@@ -295,6 +295,7 @@
         part_copies[step].start()
 
     even = lax.rem(mine, 2) == 0
+    passing = False
 
     for cut in range(cuts):
         part = rows_of_cut(cut)
@@ -319,9 +320,6 @@
         lax.fori_loop(0, seqs, pack_grad, 0, unroll=4)
         send(grad_out, grad_in, 2, cut)
 
-        if cut == 1:
-            pl.when(even)(lambda: hand_over(left))
-            pl.when(jnp.logical_not(even))(lambda: hand_over(right))
         all_of(val_out, val_in, 1, cut).wait_recv()
 
         def widen_val(at, total):
@@ -331,23 +329,29 @@
 
         total = lax.fori_loop(0, seqs, widen_val, jnp.zeros((width, points), wide), unroll=4)
         gain_out[pl.ds(begin * shares, shares)] = total.reshape(shares, own, points)
-        lax.fori_loop(0, width // 2, lambda pair, carry: cross_pair(begin * (width // 2) + pair, carry), 0, unroll=unroll)
-
-        def pack_part(at, carry):
-            for share in range(shares):
-                copy = begin * shares + share
-                part_out[copy, :, pl.ds(pl.multiple_of(at * points, points), points)] = val_wide[
-                    pl.ds(pl.multiple_of(at * group + copy * own, own), own), :
+        if cut == 1:
+            pl.when(even)(lambda: hand_over(left))
+            pl.when(jnp.logical_not(even))(lambda: hand_over(right))
+
+        away = lax.rem(mine, 2) * 2
+        for share in (dp_at(2), dp_at(left - away)) if cut == 0 else (dp_at(right + away), mine):
+            begin_pair = share * (own // 2)
+            lax.fori_loop(0, own // 2, lambda pair, carry: cross_pair(begin_pair + pair, carry), 0, unroll=unroll)
+
+            def pack_part(at, carry):
+                part_out[share, :, pl.ds(pl.multiple_of(at * points, points), points)] = val_wide[
+                    pl.ds(pl.multiple_of(at * group + share * own, own), own), :
                 ].astype(narrow)
-            return carry
-
-        lax.fori_loop(0, seqs, pack_part, 0, unroll=4)
-        if cut == 0:
-            for copy in pass_copies:
-                copy.start()
-        else:
-            pl.when(even)(lambda: hand_over(right))
-            pl.when(jnp.logical_not(even))(lambda: hand_over(left))
+                return carry
+
+            lax.fori_loop(0, seqs, pack_part, 0, unroll=4)
+            if share is not mine and cut == 1:
+                pl.when(even)(lambda: hand_over(right))
+                pl.when(jnp.logical_not(even))(lambda: hand_over(left))
+            elif cut == 0 and not passing:
+                passing = True
+                for copy in pass_copies:
+                    copy.start()
     for copy in gain_sums:
         copy.start()
     gain_in[pl.ds(mine, 1)] = gain_out[pl.ds(mine, 1)]

time: 99.5 us -> 97.5 us (0.980)
  Pallas kernels: 96.5 us -> 93.5 us
    pallas_call x1, Pallas kernels: 96.5 us -> 93.5 us  [shards(): pl.pallas_call(functools.partial(kernel, seqs, copies, cuts, scale), out_...]
where the time goes in v5:
time: 97.5 us; the launch traced here: 96.4 us
  Pallas kernels  93.5 us (96%)
  local copies, waits for them, and re-layouts  2.28 us (2%)
    pallas_call x1, Pallas kernels, shards(): pl.pallas_call(functools.partial(kernel, seqs, copies, cuts, scale), out_...  93.5 us
    unnamed x3, local copies, waits for them, and re-layouts  2.28 us

profile of v5, /device:TPU:1, one launch (start us, length us, event | category | flops | bytes accessed | tf_op | source)
XLA Modules:
  0.0 96.4 jit_solution(704163161886204681)
XLA Ops:
  0.6 93.5 %shard_map.112 = (bf16[128,4096]{1,0:T(8,128)(2,1)S(1)}, f32[8,16384]{1,0:T(8,128)S(1)}, f32[1,8]{1,0:T(1,128)S(1)}) custom-call(bf16[128,4096]{1,0:T(8,128)(2,1)} %bitcast.7, bf16[128,4096]{1,0:T(8,128)(2,1)} %bitcast.8, bf16[8,16384]{1,0:T(8,128)(2,1)} %filter_hbm.1, bf16[1,8]{1,0:T(2,128)(2,1)} %bitcast.9, bf16[256,128]{1,0:T(8,128)(2,1)} %constant.10.clone.outer_hbm, ...), custom_call_target="tpu_custom_call" | custom-call | tf_op jit(solution)/shard_map/pallas_call | solution.py:404
  94.2 1.0 %copy.15 = bf16[1,128,4096]{2,1,0:T(8,128)(2,1)} copy(bf16[1,128,4096]{2,1,0:T(8,128)(2,1)S(1)} %bitcast.5) | data formatting | bytes 2097152
  95.1 0.5 copy.17
  95.6 0.8 copy.16

commit v6 on v5

--- a/solution.py
+++ b/solution.py
@@ -13,7 +13,7 @@
 MESH = pl.DeviceIdType.MESH
 lanes = 128
 wide = jnp.float32
-unroll = 4
+unroll = 8
 narrow = jnp.bfloat16
 
 
@@ -115,7 +115,7 @@
         part = rows_of_cut(cut)
 
         def one(step, carry):
-            peer = lax.rem(me + step * 49, seqs)
+            peer = lax.rem(me + step * (49 + 30 * lax.rem(me, 2)), seqs)
             pltpu.make_async_remote_copy(
                 src_ref=rows_ref.at[peer, part],
                 dst_ref=there_ref.at[me, part],
@@ -336,7 +336,7 @@
         away = lax.rem(mine, 2) * 2
         for share in (dp_at(2), dp_at(left - away)) if cut == 0 else (dp_at(right + away), mine):
             begin_pair = share * (own // 2)
-            lax.fori_loop(0, own // 2, lambda pair, carry: cross_pair(begin_pair + pair, carry), 0, unroll=unroll)
+            lax.fori_loop(0, own // 2, lambda pair, carry: cross_pair(begin_pair + pair, carry), 0, unroll=own // 2)
 
             def pack_part(at, carry):
                 part_out[share, :, pl.ds(pl.multiple_of(at * points, points), points)] = val_wide[

time: 97.5 us -> 97.5 us (level)
  the two profiles are of different devices: /device:TPU:1 before, /device:TPU:9 now
where the time goes in v6:
time: 97.5 us; the launch traced here: 97.4 us
  Pallas kernels  94.5 us (97%)
  local copies, waits for them, and re-layouts  2.28 us (2%)
    pallas_call x1, Pallas kernels, shards(): pl.pallas_call(functools.partial(kernel, seqs, copies, cuts, scale), out_...  94.5 us
    unnamed x3, local copies, waits for them, and re-layouts  2.28 us

profile of v6, /device:TPU:9, one launch (start us, length us, event | category | flops | bytes accessed | tf_op | source)
XLA Modules:
  0.0 97.4 jit_solution(4098653453895256671)
XLA Ops:
  0.6 94.5 %shard_map.112 = (bf16[128,4096]{1,0:T(8,128)(2,1)S(1)}, f32[8,16384]{1,0:T(8,128)S(1)}, f32[1,8]{1,0:T(1,128)S(1)}) custom-call(bf16[128,4096]{1,0:T(8,128)(2,1)} %bitcast.7, bf16[128,4096]{1,0:T(8,128)(2,1)} %bitcast.8, bf16[8,16384]{1,0:T(8,128)(2,1)} %filter_hbm.1, bf16[1,8]{1,0:T(2,128)(2,1)} %bitcast.9, bf16[256,128]{1,0:T(8,128)(2,1)} %constant.10.clone.outer_hbm, ...), custom_call_target="tpu_custom_call" | custom-call | tf_op jit(solution)/shard_map/pallas_call | solution.py:404
  95.1 1.0 copy.15
  96.1 0.5 copy.17
  96.6 0.8 copy.16
